TPU v7x, 32 devices: a whole 2x2x4 slice. The times are simulated.
32 devices in a mesh: groups: 2 (over x), replica: 8 (over z, y), tensor: 2 (over core).
Axes of the slice: x: 2, y: 2, z: 4, core: 2. Of those that a mesh axis runs over, the one named last changes fastest.
Arguments:
- tokens: bfloat16 [4096, 8192], P(('groups', 'replica'), 'tensor'), parts along dimension 0, may hold values from -6 to 6
- value_weight: bfloat16 [8192, 1024], P('tensor'), may hold values from -0.0625 to 0.0625
- adapter_down: bfloat16 [256, 8192, 64], P(None, ('tensor', 'replica')), may hold values from -0.0625 to 0.0625
- adapter_up: bfloat16 [256, 64, 1024], P(None, None, 'replica'), may hold values from -0.75 to 0.75
- adapter_per_block: int32 [32], P(('groups', 'replica')), parts along dimension 0, may hold values from 0 to 255
- block_live: int32 [32], P(('groups', 'replica')), parts along dimension 0, may hold values from 1 to 128
Outputs:
- values_out: bfloat16 [4096, 1024], P(('groups', 'replica'), 'tensor'), parts along dimension 0
There are 2 independent parts, one for each index of `groups`. A program takes and returns all parts, laid end to end along the dimension named above; an argument that names none is the same for every part. Nothing has to cross between parts.
All inputs are finite; a program needn't handle non-finite values.
Results may differ from a plain program's by a relative error of at most 0.0039.
Values may be sent and summed in bfloat16 or wider, within the bound.
A program may use at most 128 MiB of HBM per device.

v0:
```python
import jax
import jax.numpy as jnp
from jax import lax
from jax.sharding import PartitionSpec as P

BLOCK = 128


def shrink_rows(features, chosen_down, count):
    block_count = count // BLOCK
    row_block = features
    row_block = row_block.reshape(block_count, BLOCK, row_block.shape[1])
    partial_sum = jnp.einsum(
        "bkf,bfr->bkr", row_block, chosen_down, preferred_element_type=jnp.float32
    )
    return partial_sum.reshape(count, chosen_down.shape[2])


def local(tokens, value_weight, adapter_down, adapter_up, adapter_per_block, block_live):
    cores = lax.axis_size("tensor")
    tok_rows = tokens.shape[0]
    rank_size = adapter_down.shape[2]
    out_width = value_weight.shape[1]
    column_halfway = out_width // cores
    owned_start_index = lax.axis_index("tensor") * column_halfway
    every_id = lax.all_gather(adapter_per_block, "replica", axis=0, tiled=True)
    base_part = jnp.dot(tokens, value_weight, preferred_element_type=jnp.float32)
    features = lax.all_to_all(tokens, "replica", split_axis=1, concat_axis=0, tiled=True)
    chosen_down = adapter_down[every_id]
    total_rows = features.shape[0]
    summed = lax.psum(shrink_rows(features, chosen_down, total_rows), ("replica", "tensor"))
    shrunk = summed.astype(jnp.bfloat16)
    chosen_up = adapter_up[every_id]
    shrunk_blocks = shrunk.reshape(-1, BLOCK, rank_size)
    column_part = jnp.einsum(
        "bkr,brc->bkc", shrunk_blocks, chosen_up, preferred_element_type=jnp.float32
    )
    column_part = column_part.reshape(total_rows, chosen_up.shape[2])
    complete_delta = lax.all_to_all(column_part, "replica", split_axis=0, concat_axis=1, tiled=True)
    adapter_delta = lax.dynamic_slice_in_dim(complete_delta, owned_start_index, column_halfway, 1)
    base_value_sum = lax.psum_scatter(base_part, "tensor", scatter_dimension=1, tiled=True)
    combined_output = base_value_sum + adapter_delta
    position = jnp.arange(BLOCK, dtype=jnp.int32)
    active_mask = (position[None, :] < block_live[:, None]).reshape(tok_rows, 1)
    return jnp.where(active_mask, combined_output, 0.0).astype(jnp.bfloat16)


def solution(mesh):
    placed = (
        P(("groups", "replica"), "tensor"),
        P("tensor", None),
        P(None, ("tensor", "replica"), None),
        P(None, None, "replica"),
        P(("groups", "replica")),
        P(("groups", "replica")),
    )
    return jax.shard_map(
        local,
        mesh=mesh,
        in_specs=placed,
        out_specs=P(("groups", "replica"), "tensor"),
        check_vma=False,
    )
```

profile of v0, /device:TPU:0, one launch (start us, length us, event | category | flops | bytes accessed | tf_op | source)
XLA Modules:
  0.0 178.7 jit_solution(8963769555877177408)
XLA Ops:
  6.5 3.1 %copy.28 = bf16[32,8,8,512]{3,2,0,1:T(8,128)(2,1)} copy(bf16[32,8,8,512]{3,2,1,0:T(8,128)(2,1)} %bitcast.39) | data formatting | bytes 4194304 | tf_op jit(solution)/shard_map/all_to_all | solution.py:28
  9.7 0.0 copy-start.3
  9.7 0.0 copy-start.1
  9.7 7.4 %all-to-all-start = ((bf16[256,8,512]{2,0,1:T(8,128)(2,1)}), bf16[256,8,512]{2,0,1:T(8,128)(2,1)S(1)}, u32[]{:S(2)}, u32[]{:S(2)}) async-start(bf16[256,8,512]{2,0,1:T(8,128)(2,1)} %bitcast.38), calls=%async_computation.1 | async-start | bytes 4194304 | tf_op jit(solution)/shard_map/all_to_all | solution.py:28
  17.1 0.0 copy-done.3
  17.1 0.6 dynamic-slice
  18.3 0.0 copy-done.1
  18.3 0.2 dynamic-update-slice
  18.6 46.9 %all-reduce = s32[16]{0:T(128)S(1)} all-reduce(s32[16]{0:T(128)S(1)} %dynamic-update-slice), channel_id=1, replica_groups=mesh['groups'=2,'replica'=8,'tensor'=2] {'replica'}, use_global_device_ids=true, to_apply=%add | all-reduce | flops 16 | bytes 128
  65.5 6.4 %gather_fusion = bf16[16,512,64]{1,2,0:T(8,128)(2,1)S(1)} fusion(bf16[256,512,64]{1,2,0:T(8,128)(2,1)} %param.8, s32[1024]{0:T(1024)S(1)} %pad_clamp_fusion), kind=kCustom, calls=%fused_computation | custom fusion | bytes 2097216 | tf_op jit(solution)/shard_map/gather | solution.py:29
  71.9 2.8 %gather_fusion.1 = bf16[16,64,128]{2,1,0:T(8,128)(2,1)S(1)} fusion(bf16[256,64,128]{2,1,0:T(8,128)(2,1)} %param.9, s32[1024]{0:T(1024)S(1)} %pad_clamp_fusion), kind=kCustom, calls=%fused_computation.1 | custom fusion | bytes 524352 | tf_op jit(solution)/shard_map/gather | solution.py:33
  74.7 0.0 all-to-all-done
  74.7 0.8 convolution_bitcast_fusion
  75.6 0.0 copy-start
  75.6 65.0 %all-reduce.2 = bf16[2048,64]{0,1:T(8,128)(2,1)S(1)} all-reduce(f32[2048,64]{0,1:T(8,128)S(1)} %bitcast.40), channel_id=1, replica_groups=mesh['groups'=2,'replica'=8,'tensor'=2] {'replica','tensor'}, use_global_device_ids=true, to_apply=%region_1.0 | all-reduce | flops 131072 | bytes 786432 | tf_op jit(solution)/shard_map/psum | solution.py:31
  140.6 1.4 fusion
  142.0 3.6 %all-to-all-start.1 = ((f32[8,256,128]{2,1,0:T(8,128)}), f32[8,256,128]{2,1,0:T(8,128)S(1)}, u32[]{:S(2)}, u32[]{:S(2)}) async-start(f32[8,256,128]{2,1,0:T(8,128)} %bitcast.5), calls=%async_computation.2 | async-start | bytes 2097152 | tf_op jit(solution)/shard_map/all_to_all | solution.py:39
  145.6 0.0 copy-start.2
  145.6 0.0 reduce-scatter.2.cloned.1.call-start
  145.6 0.0 copy-done
  145.6 6.7 %fusion.3 = f32[256,1024]{1,0:T(8,128)} fusion(bf16[256,4096]{1,0:T(8,128)(2,1)S(1)} %copy-done, bf16[4096,1024]{1,0:T(8,128)(2,1)} %param.7), kind=kOutput, calls=%fused_computation.14 | convolution fusion | flops 2147483648 | bytes 11534336 | tf_op jit(solution)/shard_map/dot_general | solution.py:27
  152.3 0.0 reduce-scatter.2.cloned.1.call-update
  152.4 0.0 copy-done.2
  152.4 0.1 compare_bitcast_fusion
  152.4 17.4 %all-to-all-done.1 = f32[8,256,128]{2,1,0:T(8,128)S(1)} async-done(((f32[8,256,128]{2,1,0:T(8,128)}), f32[8,256,128]{2,1,0:T(8,128)S(1)}, u32[]{:S(2)}, u32[]{:S(2)}) %all-to-all-start.1) | async-done | bytes 1048608 | tf_op jit(solution)/shard_map/all_to_all | solution.py:39
  169.8 0.1 copy_bitcast_fusion.1
  170.0 0.0 reduce-scatter.2.cloned.1.call-done
  170.0 1.9 %select_convert_fusion = bf16[256,512]{1,0:T(8,128)(2,1)} fusion(f32[256,512]{1,0:T(8,128)} %reduce-scatter.2.cloned.1.call-done, f32[256,1024]{1,0:T(8,128)S(1)} %copy_bitcast_fusion.1, s32[]{:T(128)S(6)} %select_n.12, pred[256]{0:T(512)(128)(4,1)S(1)} %compare_bitcast_fusion), kind=kLoop, calls=%fused_computation.6 | loop fusion | flops 393216 | bytes 1310980 | tf_op jit(solution)/shard_map/convert_element_type | solution.py:45
  (4 shorter events, 0.1 us)
Async XLA Ops:
  9.7 7.4 %copy-start.3 = (u32[32]{0:T(128)S(1)}, u32[32]{0:T(128)}, u32[]{:S(2)}) copy-start(u32[32]{0:T(128)} %constant.19) | copy-start | bytes 388
  9.7 8.7 %copy-start.1 = (s32[2]{0:T(128)S(1)}, s32[2]{0:T(128)}, u32[]{:S(2)}) copy-start(s32[2]{0:T(128)} %param.10) | copy-start | bytes 28
  9.7 65.0 %all-to-all-start = ((bf16[256,8,512]{2,0,1:T(8,128)(2,1)}), bf16[256,8,512]{2,0,1:T(8,128)(2,1)S(1)}, u32[]{:S(2)}, u32[]{:S(2)}) async-start(bf16[256,8,512]{2,0,1:T(8,128)(2,1)} %bitcast.38), calls=%async_computation.1 | async-start | bytes 4194304 | tf_op jit(solution)/shard_map/all_to_all | solution.py:28
  75.6 70.1 %copy-start = (bf16[256,4096]{1,0:T(8,128)(2,1)S(1)}, bf16[256,4096]{1,0:T(8,128)(2,1)}, u32[]{:S(2)}) copy-start(bf16[256,4096]{1,0:T(8,128)(2,1)} %param.6) | copy-start | bytes 6291460
  142.0 27.8 %all-to-all-start.1 = ((f32[8,256,128]{2,1,0:T(8,128)}), f32[8,256,128]{2,1,0:T(8,128)S(1)}, u32[]{:S(2)}, u32[]{:S(2)}) async-start(f32[8,256,128]{2,1,0:T(8,128)} %bitcast.5), calls=%async_computation.2 | async-start | bytes 2097152 | tf_op jit(solution)/shard_map/all_to_all | solution.py:39
  145.6 6.8 %copy-start.2 = (s32[2]{0:T(128)S(1)}, s32[2]{0:T(128)}, u32[]{:S(2)}) copy-start(s32[2]{0:T(128)} %param.11) | copy-start | bytes 28
  145.6 24.4 %reduce-scatter.2.cloned.1.call-start = ((), (), s32[]{:S(2)}) async-start(), calls=%async_computation.3 | async-start | bytes 1572864 | tf_op jit(solution)/shard_map/reduce_scatter | solution.py:41
Sparse Core Ops, SparseCore 0:
  152.5 9.8 reduce-scatter.1
where the time goes:
time: 179 us
  blocking collectives  112 us (63%)
  waiting for transfers between devices  17.4 us (10%)
  between operations  14.2 us (8%)
  local copies, waits for them, and re-layouts  13.3 us (7%)
  starting transfers between devices  11 us (6%)
  matrix products  8.88 us (5%)
  other arithmetic  1.94 us (1%)
    psum x1, blocking collectives, local(): lax.psum(shrink_rows(features, chosen_down, total_rows), ('replica', 'ten...  65 us
    unnamed x1, blocking collectives  46.9 us
    all_to_all x1, waiting for transfers between devices, local(): lax.all_to_all(column_part, 'replica', split_axis=0, concat_axis=1, tiled...  17.4 us
    all_to_all x1, starting transfers between devices, local(): lax.all_to_all(tokens, 'replica', split_axis=1, concat_axis=0, tiled=True)  7.41 us
    dot_general x1, matrix products, local(): jnp.dot(tokens, value_weight, preferred_element_type=jnp.float32)  6.68 us
    gather x1, local copies, waits for them, and re-layouts, local(): chosen_down = adapter_down[every_id]  6.38 us
  transfers between devices with their start and end apart: 3, of which 1 were waited for; matrix products, arithmetic and copies ran while one was open for 9% of the time, Pallas kernels for 0%

commit v1 on v0

v1 whole, which is shorter than its diff:
```python
import jax
import jax.numpy as jnp
from jax import lax
from jax.sharding import PartitionSpec as P

BLOCK = 128


def local(tokens, value_weight, adapter_down, adapter_up, adapter_per_block, block_live):
    replicas = lax.axis_size("replica")
    cores = lax.axis_size("tensor")
    core = lax.axis_index("tensor")
    rows, features = tokens.shape
    blocks = rows // BLOCK
    part, rank = adapter_down.shape[1:]
    out_width = value_weight.shape[1]
    half = out_width // cores
    every_id = lax.all_gather(adapter_per_block, "replica", axis=0, tiled=True)
    down = jnp.swapaxes(adapter_down, 1, 2)[every_id]
    down = down.reshape(replicas, blocks, rank, part)
    down = lax.all_to_all(down, "replica", split_axis=0, concat_axis=0, tiled=True)
    up = adapter_up[every_id].reshape(replicas, blocks, rank, -1)
    up = lax.all_to_all(up, "replica", split_axis=0, concat_axis=0, tiled=True)
    owners = replicas // cores
    up = lax.dynamic_slice_in_dim(up, core * owners, owners, 0)
    base = jnp.dot(tokens, value_weight, preferred_element_type=jnp.float32)
    base = lax.psum_scatter(base, "tensor", scatter_dimension=1, tiled=True)
    blocked = tokens.reshape(blocks, BLOCK, replicas, part)
    shrink = jnp.einsum("bksf,sbrf->bkr", blocked, down, preferred_element_type=jnp.float32)
    shrunk = lax.psum(shrink, "tensor").astype(jnp.bfloat16)
    delta = jnp.einsum("bkr,sbrc->bksc", shrunk, up, preferred_element_type=jnp.float32)
    combined = base + delta.reshape(rows, half)
    position = jnp.arange(BLOCK, dtype=jnp.int32)
    live = (position[None, :] < block_live[:, None]).reshape(rows, 1)
    return jnp.where(live, combined, 0.0).astype(jnp.bfloat16)


def solution(mesh):
    return jax.shard_map(
        local,
        mesh=mesh,
        in_specs=(
            P(("groups", "replica"), "tensor"),
            P("tensor", None),
            P(None, ("tensor", "replica"), None),
            P(None, None, "replica"),
            P(("groups", "replica")),
            P(("groups", "replica")),
        ),
        out_specs=P(("groups", "replica"), "tensor"),
        check_vma=False,
    )
```

time: 179 us -> 78.2 us (0.44)
  blocking collectives: 112 us -> 16.7 us
  waiting for transfers between devices: 17.4 us -> 12.3 us
  starting transfers between devices: 11 us -> 7.02 us
  local copies, waits for them, and re-layouts: 13.3 us -> 15.7 us
    psum x1, blocking collectives: 65 us -> 3.62 us  [local(): shrunk = lax.psum(shrink, 'tensor').astype(jnp.bfloat16)]
    unnamed x1, blocking collectives: 46.9 us -> 13.1 us
    all_to_all x2, waiting for transfers between devices: 17.4 us -> 12.3 us  [the longest x1 10.7 us: local(): lax.all_to_all(down, 'replica', split_axis=0, concat_axis=0, tiled=True)]
    all_to_all x2, starting transfers between devices: 11 us -> 6.98 us  [the longest x1 3.56 us: local(): lax.all_to_all(down, 'replica', split_axis=0, concat_axis=0, tiled=True)]
    unnamed x11 -> x8, local copies, waits for them, and re-layouts: 0.85 us -> 4.37 us
    all_to_all x2 -> x0, local copies, waits for them, and re-layouts: 3.24 us -> none  [the longest x1 3.13 us: local(): lax.all_to_all(tokens, 'replica', split_axis=1, concat_axis=0, tiled=True)]
    gather x2, local copies, waits for them, and re-layouts: 9.17 us -> 11 us  [the longest x1 7.52 us: local(): down = jnp.swapaxes(adapter_down, 1, 2)[every_id]]
  transfers between devices with their start and end apart: 3 -> 3, of which waited for: 1 -> 2; matrix products, arithmetic and copies ran while one was open for 9% -> 21% of each run, Pallas kernels for 0% -> 0%
where the time goes in v1:
time: 78.2 us; the launch traced here: 77.7 us
  blocking collectives  16.7 us (21%)
  local copies, waits for them, and re-layouts  15.7 us (20%)
  between operations  14.1 us (18%)
  waiting for transfers between devices  12.3 us (16%)
  matrix products  9.93 us (13%)
  starting transfers between devices  7.02 us (9%)
  other arithmetic  1.94 us (2%)
    unnamed x1, blocking collectives  13.1 us
    all_to_all x1, waiting for transfers between devices, local(): lax.all_to_all(down, 'replica', split_axis=0, concat_axis=0, tiled=True)  10.7 us
    gather x1, local copies, waits for them, and re-layouts, local(): down = jnp.swapaxes(adapter_down, 1, 2)[every_id]  7.52 us
    dot_general x1, matrix products, local(): base = jnp.dot(tokens, value_weight, preferred_element_type=jnp.float32)  6.77 us
    unnamed x8, local copies, waits for them, and re-layouts  4.37 us
    psum x1, blocking collectives, local(): shrunk = lax.psum(shrink, 'tensor').astype(jnp.bfloat16)  3.62 us
    all_to_all x1, starting transfers between devices, local(): lax.all_to_all(down, 'replica', split_axis=0, concat_axis=0, tiled=True)  3.56 us
    gather x1, local copies, waits for them, and re-layouts, local(): up = adapter_up[every_id].reshape(replicas, blocks, rank, -1)  3.47 us
  transfers between devices with their start and end apart: 3, of which 2 were waited for; matrix products, arithmetic and copies ran while one was open for 21% of the time, Pallas kernels for 0%

profile of v1, /device:TPU:0, one launch (start us, length us, event | category | flops | bytes accessed | tf_op | source)
XLA Modules:
  0.0 77.7 jit_solution(13077833921439198529)
XLA Ops:
  6.5 1.2 %dynamic-slice = u32[1]{0:T(128)} dynamic-slice(u32[32]{0:T(128)} %constant.19, u32[]{:T(128)S(6)} %add.17), dynamic_slice_sizes={1} | dynamic-slice | bytes 12
  8.4 0.9 %dynamic-update-slice = s32[16]{0:T(128)S(1)} dynamic-update-slice(s32[16]{0:T(128)S(1)} %broadcast.13, s32[2]{0:T(128)} %param.10, u32[]{:T(128)} %bitcast.2) | dynamic-update-slice | bytes 20
  9.3 13.1 %all-reduce = s32[16]{0:T(128)S(1)} all-reduce(s32[16]{0:T(128)S(1)} %dynamic-update-slice), channel_id=1, replica_groups=mesh['groups'=2,'replica'=8,'tensor'=2] {'replica'}, use_global_device_ids=true, to_apply=%add | all-reduce | flops 16 | bytes 128
  22.4 0.0 copy-start
  22.4 7.5 %gather_fusion = bf16[16,64,512]{2,1,0:T(8,128)(2,1)} fusion(bf16[256,64,512]{2,1,0:T(8,128)(2,1)} %bitcast.32, s32[1024]{0:T(1024)S(1)} %pad_clamp_fusion), kind=kCustom, calls=%fused_computation | custom fusion | bytes 2097216 | tf_op jit(solution)/shard_map/gather | solution.py:19
  29.9 3.6 %all-to-all-start = ((bf16[8,2,64,512]{3,2,1,0:T(8,128)(2,1)}), bf16[8,2,64,512]{3,2,1,0:T(8,128)(2,1)S(1)}, u32[]{:S(2)}, u32[]{:S(2)}) async-start(bf16[8,2,64,512]{3,2,1,0:T(8,128)(2,1)} %bitcast.3), calls=%async_computation.1 | async-start | bytes 2097152 | tf_op jit(solution)/shard_map/all_to_all | solution.py:21
  33.5 0.0 reduce-scatter.2.cloned.1.call-start
  33.5 0.0 copy-done
  33.5 6.8 %fusion.11 = f32[256,1024]{1,0:T(8,128)} fusion(bf16[256,4096]{1,0:T(8,128)(2,1)S(1)} %copy-done, bf16[4096,1024]{1,0:T(8,128)(2,1)} %param.7), kind=kOutput, calls=%fused_computation.16 | convolution fusion | flops 2147483648 | bytes 11534336 | tf_op jit(solution)/shard_map/dot_general | solution.py:26
  40.3 0.0 reduce-scatter.2.cloned.1.call-update
  40.3 0.0 copy-start.1
  40.3 2.3 %copy.15 = bf16[32,8,8,512]{3,2,1,0:T(8,128)(2,1)} copy(bf16[32,8,8,512]{3,1,2,0:T(8,128)(2,1)S(1)} %bitcast.30) | data formatting | bytes 4194304
  42.6 3.5 %gather_fusion.1 = bf16[16,64,128]{2,1,0:T(8,128)(2,1)} fusion(bf16[256,64,128]{2,1,0:T(8,128)(2,1)} %param.9, s32[1024]{0:T(1024)S(1)} %pad_clamp_fusion), kind=kCustom, calls=%fused_computation.1 | custom fusion | bytes 524352 | tf_op jit(solution)/shard_map/gather | solution.py:22
  46.1 10.7 %all-to-all-done = bf16[8,2,64,512]{3,2,1,0:T(8,128)(2,1)S(1)} async-done(((bf16[8,2,64,512]{3,2,1,0:T(8,128)(2,1)}), bf16[8,2,64,512]{3,2,1,0:T(8,128)(2,1)S(1)}, u32[]{:S(2)}, u32[]{:S(2)}) %all-to-all-start) | async-done | bytes 1048608 | tf_op jit(solution)/shard_map/all_to_all | solution.py:21
  56.7 3.4 %all-to-all-start.1 = ((bf16[8,2,64,128]{3,2,1,0:T(8,128)(2,1)}), bf16[8,2,64,128]{3,2,1,0:T(8,128)(2,1)S(1)}, u32[]{:S(2)}, u32[]{:S(2)}) async-start(bf16[8,2,64,128]{3,2,1,0:T(8,128)(2,1)} %bitcast.8), calls=%async_computation.2 | async-start | bytes 524288 | tf_op jit(solution)/shard_map/all_to_all | solution.py:23
  60.1 0.0 copy-done.1
  60.1 0.1 compare_bitcast_fusion
  60.2 2.9 %fusion.2 = f32[2,128,64]{1,2,0:T(8,128)S(1)} fusion(bf16[8,2,64,512]{3,2,1,0:T(8,128)(2,1)S(1)} %all-to-all-done, bf16[2,128,8,512]{3,2,1,0:T(8,128)(2,1)} %bitcast.31), kind=kOutput, calls=%fused_computation.4 | convolution fusion | flops 134217728 | bytes 3211264 | tf_op jit(solution)/shard_map/bksf,sbrf->bkr/dot_general | solution.py:29
  63.1 3.6 %psum.7 = bf16[2,128,64]{1,2,0:T(8,128)(2,1)S(1)} all-reduce(f32[2,128,64]{1,2,0:T(8,128)S(1)} %fusion.2), channel_id=1, replica_groups=mesh['groups'=2,'replica'=8,'tensor'=2] {'tensor'}, use_global_device_ids=true, to_apply=%region_1.0 | all-reduce | flops 16384 | bytes 98304 | tf_op jit(solution)/shard_map/psum | solution.py:30
  66.7 1.6 %all-to-all-done.1 = bf16[8,2,64,128]{3,2,1,0:T(8,128)(2,1)S(1)} async-done(((bf16[8,2,64,128]{3,2,1,0:T(8,128)(2,1)}), bf16[8,2,64,128]{3,2,1,0:T(8,128)(2,1)S(1)}, u32[]{:S(2)}, u32[]{:S(2)}) %all-to-all-start.1) | async-done | bytes 262176 | tf_op jit(solution)/shard_map/all_to_all | solution.py:23
  68.4 0.3 fusion.7
  68.6 0.3 copy.12
  69.0 0.0 reduce-scatter.2.cloned.1.call-done
  69.0 1.9 %fusion.6 = bf16[256,512]{1,0:T(8,128)(2,1)} fusion(f32[256,512]{1,0:T(8,128)} %reduce-scatter.2.cloned.1.call-done, f32[32,8,4,128]{3,2,1,0:T(4,128)S(1)} %bitcast.29, pred[256]{0:T(512)(128)(4,1)S(1)} %compare_bitcast_fusion), kind=kLoop, calls=%fused_computation.7 | loop fusion | flops 393216 | bytes 1310976 | tf_op jit(solution)/shard_map/convert_element_type | solution.py:35
  (3 shorter events, 0.0 us)
Async XLA Ops:
  22.4 11.1 %copy-start = (bf16[256,4096]{1,0:T(8,128)(2,1)S(1)}, bf16[256,4096]{1,0:T(8,128)(2,1)}, u32[]{:S(2)}) copy-start(bf16[256,4096]{1,0:T(8,128)(2,1)} %param.6) | copy-start | bytes 6291460
  29.9 26.8 %all-to-all-start = ((bf16[8,2,64,512]{3,2,1,0:T(8,128)(2,1)}), bf16[8,2,64,512]{3,2,1,0:T(8,128)(2,1)S(1)}, u32[]{:S(2)}, u32[]{:S(2)}) async-start(bf16[8,2,64,512]{3,2,1,0:T(8,128)(2,1)} %bitcast.3), calls=%async_computation.1 | async-start | bytes 2097152 | tf_op jit(solution)/shard_map/all_to_all | solution.py:21
  33.5 35.6 %reduce-scatter.2.cloned.1.call-start = ((), (), s32[]{:S(2)}) async-start(), calls=%async_computation.3 | async-start | bytes 1572864 | tf_op jit(solution)/shard_map/reduce_scatter | solution.py:27
  40.3 19.8 %copy-start.1 = (s32[2]{0:T(128)S(1)}, s32[2]{0:T(128)}, u32[]{:S(2)}) copy-start(s32[2]{0:T(128)} %param.11) | copy-start | bytes 28
  56.7 11.6 %all-to-all-start.1 = ((bf16[8,2,64,128]{3,2,1,0:T(8,128)(2,1)}), bf16[8,2,64,128]{3,2,1,0:T(8,128)(2,1)S(1)}, u32[]{:S(2)}, u32[]{:S(2)}) async-start(bf16[8,2,64,128]{3,2,1,0:T(8,128)(2,1)} %bitcast.8), calls=%async_computation.2 | async-start | bytes 524288 | tf_op jit(solution)/shard_map/all_to_all | solution.py:23
Sparse Core Ops, SparseCore 0:
  40.4 9.8 reduce-scatter.1

commit v2 on v1

--- a/solution.py
+++ b/solution.py
@@ -1,20 +1,301 @@
+import functools
+
 import jax
 import jax.numpy as jnp
 from jax import lax
+from jax.experimental import pallas as pl
+from jax.experimental.pallas import tpu as pltpu
 from jax.sharding import PartitionSpec as P
 
 BLOCK = 128
-
-
-def local(tokens, value_weight, adapter_down, adapter_up, adapter_per_block, block_live):
-    replicas = lax.axis_size("replica")
+LANES = 128
+TABLE_PIECES = 8
+MESH = pl.DeviceIdType.MESH
+
+
+def nearest_last(replicas):
+    middle = replicas // 2
+    return sorted(range(1, replicas), key=lambda k: (abs(k - middle), k))
+
+
+def fused_kernel(
+    replicas,
+    ids_ref,
+    tokens_hbm,
+    weight_hbm,
+    down_hbm,
+    up_hbm,
+    out_ref,
+    all_ids,
+    down_table,
+    up_table,
+    tokens,
+    weight,
+    down_out,
+    up_out,
+    down_in,
+    up_in,
+    base,
+    base_out,
+    base_in,
+    shrink_out,
+    shrink_in,
+    table_sem,
+    local_sem,
+    id_send,
+    id_recv,
+    down_send,
+    down_recv,
+    up_send,
+    up_recv,
+    pair_send,
+    pair_recv,
+):
+    me = lax.axis_index("replica")
+    core = lax.axis_index("tensor")
+    sibling = 1 - core
+    blocks = ids_ref.shape[0]
+    rank, part = down_table.shape[1:]
+    rows = tokens.shape[0]
+    half = out_ref.shape[1]
+    columns = up_table.shape[2]
+    owners = half // columns
+    offsets = nearest_last(replicas)
+    owner_core = me // owners
+
+    step = down_table.shape[0] // TABLE_PIECES
+    table_copies = [
+        pltpu.make_async_copy(
+            down_hbm.at[pl.ds(i * step, step)], down_table.at[pl.ds(i * step, step)], table_sem.at[i]
+        )
+        for i in range(TABLE_PIECES)
+    ]
+    for copy in table_copies:
+        copy.start()
+    up_copy = pltpu.make_async_copy(up_hbm, up_table, local_sem.at[0])
+    up_copy.start()
+    tokens_copy = pltpu.make_async_copy(tokens_hbm, tokens, local_sem.at[1])
+    weight_copies = [
+        pltpu.make_async_copy(
+            weight_hbm.at[:, pl.ds(c * half, half)], weight.at[:, pl.ds(c * half, half)], local_sem.at[2 + c]
+        )
+        for c in range(2)
+    ]
+
+    barrier = pltpu.get_barrier_semaphore()
+    for k in offsets:
+        pl.semaphore_signal(
+            barrier, inc=1, device_id={"replica": lax.rem(me + k, replicas)}, device_id_type=MESH
+        )
+    pl.semaphore_signal(barrier, inc=1, device_id={"tensor": sibling}, device_id_type=MESH)
+    pl.semaphore_wait(barrier, replicas)
+
+    id_copies = []
+    for k in offsets:
+        copy = pltpu.make_async_remote_copy(
+            src_ref=ids_ref,
+            dst_ref=all_ids.at[k],
+            send_sem=id_send.at[k],
+            recv_sem=id_recv.at[k],
+            device_id={"replica": lax.rem(me + k, replicas)},
+            device_id_type=MESH,
+        )
+        copy.start()
+        id_copies.append(copy)
+    for copy in table_copies:
+        copy.wait()
+    up_copy.wait()
+    tokens_copy.start()
+    for copy in weight_copies:
+        copy.start()
+    for copy in id_copies:
+        copy.wait()
+
+    down_copies, up_copies = {}, {}
+    for k in offsets:
+        peer = {"replica": lax.rem(me + k, replicas)}
+        for j in range(blocks):
+            down_out[k, j] = down_table[all_ids[replicas - k, j]]
+        down_copies[k] = pltpu.make_async_remote_copy(
+            src_ref=down_out.at[k],
+            dst_ref=down_in.at[k],
+            send_sem=down_send.at[k],
+            recv_sem=down_recv.at[k],
+            device_id=peer,
+            device_id_type=MESH,
+        )
+        down_copies[k].start()
+        up_copies[k] = pltpu.make_async_remote_copy(
+            src_ref=up_out.at[k],
+            dst_ref=up_in.at[lax.rem(me, owners)],
+            send_sem=up_send.at[k],
+            recv_sem=up_recv.at[lax.rem(me, owners)],
+            device_id=peer,
+            device_id_type=MESH,
+        )
+
+        @pl.when(owner_core == core)
+        def _():
+            for j in range(blocks):
+                up_out[k, j] = up_table[all_ids[replicas - k, j]]
+            up_copies[k].start()
+
+    for j in range(blocks):
+        down_in[0, j] = down_table[ids_ref[j]]
+
+    @pl.when(owner_core == core)
+    def _():
+        for j in range(blocks):
+            up_in[lax.rem(me, owners), j] = up_table[ids_ref[j]]
+
+    tokens_copy.wait()
+    for copy in weight_copies:
+        copy.wait()
+    tile = 256
+
+    def base_tile(column):
+        return jnp.dot(
+            tokens[...],
+            weight[:, pl.ds(pl.multiple_of(column, tile), tile)],
+            preferred_element_type=jnp.float32,
+        )
+
+    @pl.loop(0, half // tile)
+    def _(i):
+        base_out[:, pl.ds(pl.multiple_of(i * tile, tile), tile)] = base_tile(sibling * half + i * tile)
+
+    base_copy = pltpu.make_async_remote_copy(
+        src_ref=base_out,
+        dst_ref=base_in,
+        send_sem=pair_send.at[0],
+        recv_sem=pair_recv.at[0],
+        device_id={"tensor": sibling},
+        device_id_type=MESH,
+    )
+    base_copy.start()
+
+    @pl.loop(0, half // tile)
+    def _(i):
+        base[:, pl.ds(pl.multiple_of(i * tile, tile), tile)] = base_tile(core * half + i * tile)
+
+    def add_part(k, first):
+        column = pl.multiple_of(lax.rem(me + replicas - k, replicas) * part, LANES)
+        for j in range(blocks):
+            span = pl.ds(j * BLOCK, BLOCK)
+            term = lax.dot_general(
+                tokens[span, pl.ds(column, part)],
+                down_in[k, j],
+                (((1,), (1,)), ((), ())),
+                preferred_element_type=jnp.float32,
+            )
+            shrink_out[span, :] = term if first else shrink_out[span, :] + term
+
+    add_part(0, True)
+    base_copy.wait()
+    base[...] += base_in[...]
+    for k in reversed(offsets):
+        down_copies[k].wait_recv()
+        add_part(k, False)
+
+    shrink_copy = pltpu.make_async_remote_copy(
+        src_ref=shrink_out,
+        dst_ref=shrink_in,
+        send_sem=pair_send.at[1],
+        recv_sem=pair_recv.at[1],
+        device_id={"tensor": sibling},
+        device_id_type=MESH,
+    )
+    shrink_copy.start()
+    for s in range(owners):
+        arriving = pltpu.make_async_remote_copy(
+            src_ref=up_out.at[0],
+            dst_ref=up_in.at[s],
+            send_sem=up_send.at[0],
+            recv_sem=up_recv.at[s],
+            device_id={"replica": lax.rem(me + 1, replicas)},
+            device_id_type=MESH,
+        )
+
+        @pl.when(core * owners + s != me)
+        def _():
+            arriving.wait_recv()
+
+    shrink_copy.wait()
+    shrunk = (shrink_out[...] + shrink_in[...]).astype(jnp.bfloat16)
+    for s in range(owners):
+        for j in range(blocks):
+            span = pl.ds(j * BLOCK, BLOCK)
+            delta = jnp.dot(
+                shrunk[j * BLOCK : (j + 1) * BLOCK], up_in[s, j], preferred_element_type=jnp.float32
+            )
+            wide = pl.ds(s * columns, columns)
+            out_ref[span, wide] = (base[span, wide] + delta).astype(out_ref.dtype)
+
+    for k in offsets:
+        down_copies[k].wait_send()
+
+    @pl.when(owner_core == core)
+    def _():
+        for k in offsets:
+            up_copies[k].wait_send()
+
+
+def fused(replicas, tokens, value_weight, adapter_down, adapter_up, adapter_per_block):
+    rows, features = tokens.shape
+    adapters, part, rank = adapter_down.shape
+    blocks = rows // BLOCK
+    out_width = value_weight.shape[1]
+    half = out_width // 2
+    columns = adapter_up.shape[2]
+    owners = half // columns
+    dma = pltpu.SemaphoreType.DMA
+    return pl.pallas_call(
+        functools.partial(fused_kernel, replicas),
+        out_shape=jax.ShapeDtypeStruct((rows, half), jnp.bfloat16),
+        in_specs=[pl.BlockSpec(memory_space=pltpu.SMEM)] + [pl.BlockSpec(memory_space=pl.ANY)] * 4,
+        out_specs=pl.BlockSpec(memory_space=pltpu.VMEM),
+        scratch_shapes=[
+            pltpu.SMEM((replicas, blocks), jnp.int32),
+            pltpu.VMEM((adapters, rank, part), jnp.bfloat16),
+            pltpu.VMEM((adapters, rank, columns), jnp.bfloat16),
+            pltpu.VMEM((rows, features), jnp.bfloat16),
+            pltpu.VMEM((features, out_width), jnp.bfloat16),
+            pltpu.VMEM((replicas, blocks, rank, part), jnp.bfloat16),
+            pltpu.VMEM((replicas, blocks, rank, columns), jnp.bfloat16),
+            pltpu.VMEM((replicas, blocks, rank, part), jnp.bfloat16),
+            pltpu.VMEM((owners, blocks, rank, columns), jnp.bfloat16),
+            pltpu.VMEM((rows, half), jnp.float32),
+            pltpu.VMEM((rows, half), jnp.float32),
+            pltpu.VMEM((rows, half), jnp.float32),
+            pltpu.VMEM((rows, rank), jnp.float32),
+            pltpu.VMEM((rows, rank), jnp.float32),
+            dma((TABLE_PIECES,)),
+            dma((4,)),
+            dma((replicas,)),
+            dma((replicas,)),
+            dma((replicas,)),
+            dma((replicas,)),
+            dma((replicas,)),
+            dma((owners,)),
+            dma((2,)),
+            dma((2,)),
+        ],
+        compiler_params=pltpu.CompilerParams(
+            collective_id=0, has_side_effects=True, vmem_limit_bytes=56 * 1024 * 1024
+        ),
+        cost_estimate=pl.CostEstimate(
+            flops=2 * rows * features * (out_width + rank), bytes_accessed=32 * 1024 * 1024, transcendentals=0
+        ),
+    )(adapter_per_block, tokens, value_weight, jnp.swapaxes(adapter_down, 1, 2), adapter_up)
+
+
+def spread(replicas, tokens, value_weight, adapter_down, adapter_up, adapter_per_block):
     cores = lax.axis_size("tensor")
     core = lax.axis_index("tensor")
-    rows, features = tokens.shape
+    rows = tokens.shape[0]
     blocks = rows // BLOCK
     part, rank = adapter_down.shape[1:]
-    out_width = value_weight.shape[1]
-    half = out_width // cores
+    half = value_weight.shape[1] // cores
     every_id = lax.all_gather(adapter_per_block, "replica", axis=0, tiled=True)
     down = jnp.swapaxes(adapter_down, 1, 2)[every_id]
     down = down.reshape(replicas, blocks, rank, part)
@@ -29,10 +310,20 @@
     shrink = jnp.einsum("bksf,sbrf->bkr", blocked, down, preferred_element_type=jnp.float32)
     shrunk = lax.psum(shrink, "tensor").astype(jnp.bfloat16)
     delta = jnp.einsum("bkr,sbrc->bksc", shrunk, up, preferred_element_type=jnp.float32)
-    combined = base + delta.reshape(rows, half)
+    return base + delta.reshape(rows, half)
+
+
+def local(tokens, value_weight, adapter_down, adapter_up, adapter_per_block, block_live):
+    replicas = lax.axis_size("replica")
+    cores = lax.axis_size("tensor")
+    half = value_weight.shape[1] // cores
+    part, columns = adapter_down.shape[1], adapter_up.shape[2]
+    aligned = part % LANES == 0 and columns % LANES == 0 and half % 256 == 0
+    inner = fused if aligned and cores == 2 and half % columns == 0 else spread
+    combined = inner(replicas, tokens, value_weight, adapter_down, adapter_up, adapter_per_block)
     position = jnp.arange(BLOCK, dtype=jnp.int32)
-    live = (position[None, :] < block_live[:, None]).reshape(rows, 1)
-    return jnp.where(live, combined, 0.0).astype(jnp.bfloat16)
+    live = (position[None, :] < block_live[:, None]).reshape(tokens.shape[0], 1)
+    return jnp.where(live, combined, 0).astype(jnp.bfloat16)
 
 
 def solution(mesh):

time: 78.2 us -> 42 us (0.54)
  the two profiles are of different devices: /device:TPU:0 before, /device:TPU:15 now
where the time goes in v2:
time: 42 us; the launch traced here: 41.8 us
  Pallas kernels  39.3 us (94%)
  other arithmetic  2.48 us (6%)
    pallas_call x1, Pallas kernels, fused(): pl.pallas_call(functools.partial(fused_kernel, replicas), out_shape=jax.S...  39.3 us
    select_n x1, other arithmetic, local(): return jnp.where(live, combined, 0).astype(jnp.bfloat16)  1.76 us

profile of v2, /device:TPU:15, one launch (start us, length us, event | category | flops | bytes accessed | tf_op | source)
XLA Modules:
  0.0 41.8 jit_solution(17002460704155926404)
XLA Ops:
  0.0 0.7 %compare_bitcast_fusion = pred[256]{0:T(512)(128)(4,1)S(1)} fusion(s32[2]{0:T(128)} %param.11), kind=kLoop, calls=%fused_computation.1 | loop fusion | flops 256 | bytes 264 | tf_op jit(solution)/shard_map/lt | solution.py:325
  0.7 39.3 %shard_map.64 = bf16[256,512]{1,0:T(8,128)(2,1)} custom-call(s32[2]{0:T(128)} %ids_ref.1, bf16[256,4096]{1,0:T(8,128)(2,1)} %tokens_hbm.1, bf16[4096,1024]{1,0:T(8,128)(2,1)} %weight_hbm.1, bf16[256,64,512]{2,1,0:T(8,128)(2,1)} %bitcast.3, bf16[256,64,128]{2,1,0:T(8,128)(2,1)} %up_hbm.1), custom_call_target="tpu_custom_call" | custom-call | flops 2281701376 | bytes 33554432 | tf_op jit(solution)/shard_map/pallas_call | solution.py:252
  40.0 1.8 %broadcast_select_fusion = bf16[256,512]{1,0:T(8,128)(2,1)} fusion(bf16[256,512]{1,0:T(8,128)(2,1)} %shard_map.64, pred[256]{0:T(512)(128)(4,1)S(1)} %compare_bitcast_fusion), kind=kLoop, calls=%fused_computation | loop fusion | flops 131072 | bytes 524544 | tf_op jit(solution)/shard_map/jit(_where)/select_n | solution.py:326

commit v3 on v2

--- a/solution.py
+++ b/solution.py
@@ -9,25 +9,28 @@
 
 BLOCK = 128
 LANES = 128
-TABLE_PIECES = 8
+CUTS = ((0, 1), (1, 3))
 MESH = pl.DeviceIdType.MESH
 
 
-def nearest_last(replicas):
+def partners(replicas, me):
     middle = replicas // 2
-    return sorted(range(1, replicas), key=lambda k: (abs(k - middle), k))
+    order = [*range(middle - 1, middle + 2), *range(middle - 2, 0, -1), *range(middle + 2, replicas)]
+    return [(k, lax.rem(me + k, replicas), lax.rem(me + replicas - k, replicas)) for k in order]
 
 
 def fused_kernel(
     replicas,
     ids_ref,
+    live_ref,
     tokens_hbm,
     weight_hbm,
     down_hbm,
     up_hbm,
     out_ref,
     all_ids,
-    down_table,
+    head_table,
+    tail_table,
     up_table,
     tokens,
     weight,
@@ -55,25 +58,25 @@
     core = lax.axis_index("tensor")
     sibling = 1 - core
     blocks = ids_ref.shape[0]
-    rank, part = down_table.shape[1:]
+    rank, part = down_in.shape[2:]
     rows = tokens.shape[0]
     half = out_ref.shape[1]
     columns = up_table.shape[2]
     owners = half // columns
-    offsets = nearest_last(replicas)
+    peers = partners(replicas, me)
     owner_core = me // owners
 
-    step = down_table.shape[0] // TABLE_PIECES
+    cuts = [(cut * rank // 4, size * rank // 4) for cut, size in CUTS]
+    tables = [head_table, tail_table]
     table_copies = [
         pltpu.make_async_copy(
-            down_hbm.at[pl.ds(i * step, step)], down_table.at[pl.ds(i * step, step)], table_sem.at[i]
-        )
-        for i in range(TABLE_PIECES)
+            down_hbm.at[:, pl.ds(cut, size)], tables[i], table_sem.at[i]
+        )
+        for i, (cut, size) in enumerate(cuts)
     ]
     for copy in table_copies:
         copy.start()
     up_copy = pltpu.make_async_copy(up_hbm, up_table, local_sem.at[0])
-    up_copy.start()
     tokens_copy = pltpu.make_async_copy(tokens_hbm, tokens, local_sem.at[1])
     weight_copies = [
         pltpu.make_async_copy(
@@ -83,68 +86,72 @@
     ]
 
     barrier = pltpu.get_barrier_semaphore()
-    for k in offsets:
-        pl.semaphore_signal(
-            barrier, inc=1, device_id={"replica": lax.rem(me + k, replicas)}, device_id_type=MESH
-        )
+    for _, to, _ in peers:
+        pl.semaphore_signal(barrier, inc=1, device_id={"replica": to}, device_id_type=MESH)
     pl.semaphore_signal(barrier, inc=1, device_id={"tensor": sibling}, device_id_type=MESH)
     pl.semaphore_wait(barrier, replicas)
 
     id_copies = []
-    for k in offsets:
+    for k, to, _ in peers:
         copy = pltpu.make_async_remote_copy(
             src_ref=ids_ref,
             dst_ref=all_ids.at[k],
             send_sem=id_send.at[k],
             recv_sem=id_recv.at[k],
-            device_id={"replica": lax.rem(me + k, replicas)},
+            device_id={"replica": to},
             device_id_type=MESH,
         )
         copy.start()
         id_copies.append(copy)
-    for copy in table_copies:
+    for copy in id_copies:
         copy.wait()
-    up_copy.wait()
+
+    down_copies, up_copies = {}, {}
+    for i, (cut, size) in enumerate(cuts):
+        table_copies[i].wait()
+        span = pl.ds(cut, size)
+        for k, to, _ in peers:
+            for j in range(blocks):
+                down_out[k, j, span] = tables[i][all_ids[replicas - k, j]]
+            down_copies[k, i] = pltpu.make_async_remote_copy(
+                src_ref=down_out.at[k, :, span],
+                dst_ref=down_in.at[k, :, span],
+                send_sem=down_send.at[k, i],
+                recv_sem=down_recv.at[k, i],
+                device_id={"replica": to},
+                device_id_type=MESH,
+            )
+            down_copies[k, i].start()
+
+    @pl.when(owner_core == core)
+    def _():
+        up_copy.start()
+
     tokens_copy.start()
     for copy in weight_copies:
         copy.start()
-    for copy in id_copies:
-        copy.wait()
-
-    down_copies, up_copies = {}, {}
-    for k in offsets:
-        peer = {"replica": lax.rem(me + k, replicas)}
-        for j in range(blocks):
-            down_out[k, j] = down_table[all_ids[replicas - k, j]]
-        down_copies[k] = pltpu.make_async_remote_copy(
-            src_ref=down_out.at[k],
-            dst_ref=down_in.at[k],
-            send_sem=down_send.at[k],
-            recv_sem=down_recv.at[k],
-            device_id=peer,
-            device_id_type=MESH,
-        )
-        down_copies[k].start()
+
+    for j in range(blocks):
+        for table, (cut, size) in zip(tables, cuts):
+            down_in[0, j, pl.ds(cut, size)] = table[ids_ref[j]]
+
+    for k, to, _ in peers:
         up_copies[k] = pltpu.make_async_remote_copy(
             src_ref=up_out.at[k],
             dst_ref=up_in.at[lax.rem(me, owners)],
             send_sem=up_send.at[k],
             recv_sem=up_recv.at[lax.rem(me, owners)],
-            device_id=peer,
+            device_id={"replica": to},
             device_id_type=MESH,
         )
 
-        @pl.when(owner_core == core)
-        def _():
+    @pl.when(owner_core == core)
+    def _():
+        up_copy.wait()
+        for k, _, _ in peers:
             for j in range(blocks):
                 up_out[k, j] = up_table[all_ids[replicas - k, j]]
             up_copies[k].start()
-
-    for j in range(blocks):
-        down_in[0, j] = down_table[ids_ref[j]]
-
-    @pl.when(owner_core == core)
-    def _():
         for j in range(blocks):
             up_in[lax.rem(me, owners), j] = up_table[ids_ref[j]]
 
@@ -178,8 +185,8 @@
     def _(i):
         base[:, pl.ds(pl.multiple_of(i * tile, tile), tile)] = base_tile(core * half + i * tile)
 
-    def add_part(k, first):
-        column = pl.multiple_of(lax.rem(me + replicas - k, replicas) * part, LANES)
+    def add_part(k, source, first):
+        column = pl.multiple_of(source * part, LANES)
         for j in range(blocks):
             span = pl.ds(j * BLOCK, BLOCK)
             term = lax.dot_general(
@@ -190,12 +197,13 @@
             )
             shrink_out[span, :] = term if first else shrink_out[span, :] + term
 
-    add_part(0, True)
+    add_part(0, me, True)
     base_copy.wait()
     base[...] += base_in[...]
-    for k in reversed(offsets):
-        down_copies[k].wait_recv()
-        add_part(k, False)
+    for k, _, source in peers[::-1]:
+        for i in range(len(cuts)):
+            down_copies[k, i].wait_recv()
+        add_part(k, source, False)
 
     shrink_copy = pltpu.make_async_remote_copy(
         src_ref=shrink_out,
@@ -229,18 +237,20 @@
                 shrunk[j * BLOCK : (j + 1) * BLOCK], up_in[s, j], preferred_element_type=jnp.float32
             )
             wide = pl.ds(s * columns, columns)
-            out_ref[span, wide] = (base[span, wide] + delta).astype(out_ref.dtype)
-
-    for k in offsets:
-        down_copies[k].wait_send()
+            position = lax.broadcasted_iota(jnp.int32, delta.shape, 0)
+            value = jnp.where(position < live_ref[j], base[span, wide] + delta, 0.0)
+            out_ref[span, wide] = value.astype(out_ref.dtype)
+
+    for copy in down_copies.values():
+        copy.wait_send()
 
     @pl.when(owner_core == core)
     def _():
-        for k in offsets:
-            up_copies[k].wait_send()
-
-
-def fused(replicas, tokens, value_weight, adapter_down, adapter_up, adapter_per_block):
+        for copy in up_copies.values():
+            copy.wait_send()
+
+
+def fused(replicas, tokens, value_weight, adapter_down, adapter_up, adapter_per_block, block_live):
     rows, features = tokens.shape
     adapters, part, rank = adapter_down.shape
     blocks = rows // BLOCK
@@ -252,11 +262,11 @@
     return pl.pallas_call(
         functools.partial(fused_kernel, replicas),
         out_shape=jax.ShapeDtypeStruct((rows, half), jnp.bfloat16),
-        in_specs=[pl.BlockSpec(memory_space=pltpu.SMEM)] + [pl.BlockSpec(memory_space=pl.ANY)] * 4,
+        in_specs=[pl.BlockSpec(memory_space=pltpu.SMEM)] * 2 + [pl.BlockSpec(memory_space=pl.ANY)] * 4,
         out_specs=pl.BlockSpec(memory_space=pltpu.VMEM),
         scratch_shapes=[
             pltpu.SMEM((replicas, blocks), jnp.int32),
-            pltpu.VMEM((adapters, rank, part), jnp.bfloat16),
+            *[pltpu.VMEM((adapters, size * rank // 4, part), jnp.bfloat16) for _, size in CUTS],
             pltpu.VMEM((adapters, rank, columns), jnp.bfloat16),
             pltpu.VMEM((rows, features), jnp.bfloat16),
             pltpu.VMEM((features, out_width), jnp.bfloat16),
@@ -269,12 +279,12 @@
             pltpu.VMEM((rows, half), jnp.float32),
             pltpu.VMEM((rows, rank), jnp.float32),
             pltpu.VMEM((rows, rank), jnp.float32),
-            dma((TABLE_PIECES,)),
+            dma((len(CUTS),)),
             dma((4,)),
             dma((replicas,)),
             dma((replicas,)),
-            dma((replicas,)),
-            dma((replicas,)),
+            dma((replicas, len(CUTS))),
+            dma((replicas, len(CUTS))),
             dma((replicas,)),
             dma((owners,)),
             dma((2,)),
@@ -286,10 +296,10 @@
         cost_estimate=pl.CostEstimate(
             flops=2 * rows * features * (out_width + rank), bytes_accessed=32 * 1024 * 1024, transcendentals=0
         ),
-    )(adapter_per_block, tokens, value_weight, jnp.swapaxes(adapter_down, 1, 2), adapter_up)
-
-
-def spread(replicas, tokens, value_weight, adapter_down, adapter_up, adapter_per_block):
+    )(adapter_per_block, block_live, tokens, value_weight, jnp.swapaxes(adapter_down, 1, 2), adapter_up)
+
+
+def spread(replicas, tokens, value_weight, adapter_down, adapter_up, adapter_per_block, block_live):
     cores = lax.axis_size("tensor")
     core = lax.axis_index("tensor")
     rows = tokens.shape[0]
@@ -310,7 +320,10 @@
     shrink = jnp.einsum("bksf,sbrf->bkr", blocked, down, preferred_element_type=jnp.float32)
     shrunk = lax.psum(shrink, "tensor").astype(jnp.bfloat16)
     delta = jnp.einsum("bkr,sbrc->bksc", shrunk, up, preferred_element_type=jnp.float32)
-    return base + delta.reshape(rows, half)
+    combined = base + delta.reshape(rows, half)
+    position = jnp.arange(BLOCK, dtype=jnp.int32)
+    live = (position[None, :] < block_live[:, None]).reshape(rows, 1)
+    return jnp.where(live, combined, 0.0).astype(jnp.bfloat16)
 
 
 def local(tokens, value_weight, adapter_down, adapter_up, adapter_per_block, block_live):
@@ -319,11 +332,9 @@
     half = value_weight.shape[1] // cores
     part, columns = adapter_down.shape[1], adapter_up.shape[2]
     aligned = part % LANES == 0 and columns % LANES == 0 and half % 256 == 0
+    aligned = aligned and replicas >= 4 and adapter_down.shape[2] % 64 == 0
     inner = fused if aligned and cores == 2 and half % columns == 0 else spread
-    combined = inner(replicas, tokens, value_weight, adapter_down, adapter_up, adapter_per_block)
-    position = jnp.arange(BLOCK, dtype=jnp.int32)
-    live = (position[None, :] < block_live[:, None]).reshape(tokens.shape[0], 1)
-    return jnp.where(live, combined, 0).astype(jnp.bfloat16)
+    return inner(replicas, tokens, value_weight, adapter_down, adapter_up, adapter_per_block, block_live)
 
 
 def solution(mesh):

time: 42 us -> 39.7 us (0.945)
  other arithmetic: 2.48 us -> 0 us
  local copies, waits for them, and re-layouts: 0 us -> 1.67 us
  Pallas kernels: 39.3 us -> 37.8 us
    select_n x1 -> x0, other arithmetic: 1.76 us -> none  [local(): return jnp.where(live, combined, 0).astype(jnp.bfloat16)]
    unnamed x0 -> x1, local copies, waits for them, and re-layouts: none -> 1.67 us
    pallas_call x1, Pallas kernels: 39.3 us -> 37.8 us  [fused(): pl.pallas_call(functools.partial(fused_kernel, replicas), out_shape=jax.S...]
    lt x1 -> x0, other arithmetic: 0.73 us -> none  [local(): live = (position[None, :] < block_live[:, None]).reshape(tokens.shape[0], 1)]
where the time goes in v3:
time: 39.7 us; the launch traced here: 39.5 us
  Pallas kernels  37.8 us (95%)
  local copies, waits for them, and re-layouts  1.67 us (4%)
    pallas_call x1, Pallas kernels, fused(): pl.pallas_call(functools.partial(fused_kernel, replicas), out_shape=jax.S...  37.8 us
    unnamed x1, local copies, waits for them, and re-layouts  1.67 us

profile of v3, /device:TPU:15, one launch (start us, length us, event | category | flops | bytes accessed | tf_op | source)
XLA Modules:
  0.0 39.5 jit_solution(6382172235431679390)
XLA Ops:
  0.0 37.8 %shard_map.64 = bf16[256,512]{1,0:T(8,128)(2,1)} custom-call(s32[2]{0:T(128)} %ids_ref.1, s32[2]{0:T(128)} %live_ref.1, bf16[256,4096]{1,0:T(8,128)(2,1)} %tokens_hbm.1, bf16[4096,1024]{1,0:T(8,128)(2,1)} %weight_hbm.1, bf16[256,64,512]{2,1,0:T(8,128)(2,1)} %bitcast.1, bf16[256,64,128]{2,1,0:T(8,128)(2,1)} %up_hbm.1), custom_call_target="tpu_custom_call" | custom-call | flops 2281701376 | bytes 33554432 | tf_op jit(solution)/shard_map/pallas_call | solution.py:262
  37.8 1.7 %copy.8 = bf16[256,512]{1,0:T(8,128)(2,1)} copy(bf16[256,512]{1,0:T(8,128)(2,1)} %shard_map.64) | data formatting | bytes 524288

commit v4 on v3

--- a/solution.py
+++ b/solution.py
@@ -9,7 +9,7 @@
 
 BLOCK = 128
 LANES = 128
-CUTS = ((0, 1), (1, 3))
+CUTS = ((0, 2), (2, 2))
 MESH = pl.DeviceIdType.MESH
 
 
@@ -185,7 +185,7 @@
     def _(i):
         base[:, pl.ds(pl.multiple_of(i * tile, tile), tile)] = base_tile(core * half + i * tile)
 
-    def add_part(k, source, first):
+    def add_part(k, source, first, finish=lambda j: None):
         column = pl.multiple_of(source * part, LANES)
         for j in range(blocks):
             span = pl.ds(j * BLOCK, BLOCK)
@@ -196,24 +196,31 @@
                 preferred_element_type=jnp.float32,
             )
             shrink_out[span, :] = term if first else shrink_out[span, :] + term
+            finish(j)
 
     add_part(0, me, True)
     base_copy.wait()
     base[...] += base_in[...]
-    for k, _, source in peers[::-1]:
+    shrink_copies = [
+        pltpu.make_async_remote_copy(
+            src_ref=shrink_out.at[pl.ds(j * BLOCK, BLOCK)],
+            dst_ref=shrink_in.at[pl.ds(j * BLOCK, BLOCK)],
+            send_sem=pair_send.at[1 + j],
+            recv_sem=pair_recv.at[1 + j],
+            device_id={"tensor": sibling},
+            device_id_type=MESH,
+        )
+        for j in range(blocks)
+    ]
+    for k, _, source in peers[:0:-1]:
         for i in range(len(cuts)):
             down_copies[k, i].wait_recv()
         add_part(k, source, False)
-
-    shrink_copy = pltpu.make_async_remote_copy(
-        src_ref=shrink_out,
-        dst_ref=shrink_in,
-        send_sem=pair_send.at[1],
-        recv_sem=pair_recv.at[1],
-        device_id={"tensor": sibling},
-        device_id_type=MESH,
-    )
-    shrink_copy.start()
+    k, _, source = peers[0]
+    for i in range(len(cuts)):
+        down_copies[k, i].wait_recv()
+    add_part(k, source, False, lambda j: shrink_copies[j].start())
+
     for s in range(owners):
         arriving = pltpu.make_async_remote_copy(
             src_ref=up_out.at[0],
@@ -228,14 +235,12 @@
         def _():
             arriving.wait_recv()
 
-    shrink_copy.wait()
-    shrunk = (shrink_out[...] + shrink_in[...]).astype(jnp.bfloat16)
-    for s in range(owners):
-        for j in range(blocks):
-            span = pl.ds(j * BLOCK, BLOCK)
-            delta = jnp.dot(
-                shrunk[j * BLOCK : (j + 1) * BLOCK], up_in[s, j], preferred_element_type=jnp.float32
-            )
+    for j in range(blocks):
+        span = pl.ds(j * BLOCK, BLOCK)
+        shrink_copies[j].wait()
+        shrunk = (shrink_out[span, :] + shrink_in[span, :]).astype(jnp.bfloat16)
+        for s in range(owners):
+            delta = jnp.dot(shrunk, up_in[s, j], preferred_element_type=jnp.float32)
             wide = pl.ds(s * columns, columns)
             position = lax.broadcasted_iota(jnp.int32, delta.shape, 0)
             value = jnp.where(position < live_ref[j], base[span, wide] + delta, 0.0)
@@ -287,8 +292,8 @@
             dma((replicas, len(CUTS))),
             dma((replicas,)),
             dma((owners,)),
-            dma((2,)),
-            dma((2,)),
+            dma((1 + blocks,)),
+            dma((1 + blocks,)),
         ],
         compiler_params=pltpu.CompilerParams(
             collective_id=0, has_side_effects=True, vmem_limit_bytes=56 * 1024 * 1024

time: 39.7 us -> 39.4 us (level)
  no operation moved by 1% of the time
where the time goes in v4:
time: 39.4 us; the launch traced here: 39.2 us
  Pallas kernels  37.6 us (95%)
  local copies, waits for them, and re-layouts  1.67 us (4%)
    pallas_call x1, Pallas kernels, fused(): pl.pallas_call(functools.partial(fused_kernel, replicas), out_shape=jax.S...  37.6 us
    unnamed x1, local copies, waits for them, and re-layouts  1.67 us

profile of v4, /device:TPU:15, one launch (start us, length us, event | category | flops | bytes accessed | tf_op | source)
XLA Modules:
  0.0 39.2 jit_solution(5429383509046842306)
XLA Ops:
  0.0 37.6 %shard_map.64 = bf16[256,512]{1,0:T(8,128)(2,1)} custom-call(s32[2]{0:T(128)} %ids_ref.1, s32[2]{0:T(128)} %live_ref.1, bf16[256,4096]{1,0:T(8,128)(2,1)} %tokens_hbm.1, bf16[4096,1024]{1,0:T(8,128)(2,1)} %weight_hbm.1, bf16[256,64,512]{2,1,0:T(8,128)(2,1)} %bitcast.1, bf16[256,64,128]{2,1,0:T(8,128)(2,1)} %up_hbm.1), custom_call_target="tpu_custom_call" | custom-call | flops 2281701376 | bytes 33554432 | tf_op jit(solution)/shard_map/pallas_call | solution.py:267
  37.6 1.7 %copy.8 = bf16[256,512]{1,0:T(8,128)(2,1)} copy(bf16[256,512]{1,0:T(8,128)(2,1)} %shard_map.64) | data formatting | bytes 524288
